TPU v7x, 32 devices: a whole 2x2x4 slice. The times are simulated.
32 devices in a mesh: pipe: 8 (over z, x), ctx: 4 (over y, core).
Axes of the slice: x: 2, y: 2, z: 4, core: 2. Of those that a mesh axis runs over, the one named last changes fastest.
Arguments:
- forward_in: bfloat16 [8, 2, 512, 8192], P('pipe', None, 'ctx'), may hold values from -8 to 8
- backward_in: bfloat16 [8, 2, 512, 8192], P('pipe', None, 'ctx'), may hold values from -8 to 8
- grad_out: bfloat16 [8, 2, 512, 8192], P('pipe', None, 'ctx'), may hold values from -6 to 6
- cached_keys: bfloat16 [8, 2, 512, 8, 128], P('pipe', None, 'ctx'), may hold values from -21 to 21
- cached_values: bfloat16 [8, 2, 512, 8, 128], P('pipe', None, 'ctx'), may hold values from -6 to 6
- norm_gain: float32 [8, 2, 8192], P('pipe'), may hold values from 0.25 to 1.75
- key_weight: bfloat16 [8, 2, 8192, 1024], P('pipe', None, 'ctx'), may hold values from -0.0625 to 0.0625
- value_weight: bfloat16 [8, 2, 8192, 1024], P('pipe', None, 'ctx'), may hold values from -0.0625 to 0.0625
- segment_index: int32 [8, 2, 2], P('pipe'), may hold values from 0 to 1, as said below
Outputs:
- next_forward: bfloat16 [8, 2, 512, 8192], P('pipe', None, 'ctx')
- next_backward: bfloat16 [8, 2, 512, 8192], P('pipe', None, 'ctx')
Inputs may be any that keep to these rules, and one draw needn't show every extreme that they name: `segment_index`: the largest segment index, 1, occurs in every draw.
All inputs are finite; a program needn't handle non-finite values.
Results may differ from a plain program's by a relative error of at most 0.04.
Values may be sent and summed in bfloat16 or wider, within the bound.
A program may use at most 256 MiB of HBM per device.

v0:
```python
import jax
import jax.numpy as jnp
from jax import lax
from jax.sharding import PartitionSpec as P

NEGATIVE = -1e30


def passed_along(array, axis, by):
    count = lax.axis_size(axis)
    return lax.ppermute(array, axis, [(i, (i + by) % count) for i in range(count)])


def normalize(in_rows, gain_row):
    as_float = in_rows.astype(jnp.float32)
    inverse = lax.rsqrt(jnp.mean(as_float * as_float, axis=-1, keepdims=True) + 1e-05)
    normed = as_float * inverse
    return (normed, inverse, (normed * gain_row).astype(jnp.bfloat16))


def probabilities(queries, key_list, position, cache_len):
    seg_len = queries.shape[0]
    factor = queries.shape[-1] ** (-0.5)
    scores = (
        jnp.einsum("tkgd,skd->kgts", queries, key_list, preferred_element_type=jnp.float32) * factor
    )
    column = lax.broadcasted_iota(jnp.int32, (seg_len, key_list.shape[0]), 1)
    row_ids = lax.broadcasted_iota(jnp.int32, (seg_len, key_list.shape[0]), 0)
    visible = jnp.where(
        column < cache_len, column < position * seg_len, column - cache_len <= row_ids
    )
    scores = jnp.where(visible, scores, NEGATIVE)
    row_max = jnp.max(scores, axis=-1, keepdims=True)
    lifted = jnp.exp(scores - row_max)
    return lifted / jnp.sum(lifted, axis=-1, keepdims=True)


def attend(queries, key_list, value_list, position, cache_len):
    prob_full = probabilities(queries, key_list, position, cache_len)
    prob_half = prob_full.astype(jnp.bfloat16)
    attended = jnp.einsum(
        "kgts,skd->tkgd", prob_half, value_list, preferred_element_type=jnp.float32
    )
    return (prob_full, prob_half, attended.astype(jnp.bfloat16))


def attend_back(queries, key_list, value_list, position, cache_len, grad_heads):
    prob_full, prob_half, attended = attend(queries, key_list, value_list, position, cache_len)
    grad_prob = jnp.einsum(
        "tkgd,skd->kgts", grad_heads, value_list, preferred_element_type=jnp.float32
    )
    row_delta = jnp.sum(grad_heads.astype(jnp.float32) * attended.astype(jnp.float32), axis=-1)
    row_delta = jnp.transpose(row_delta, (1, 2, 0))[..., None]
    factor = queries.shape[-1] ** (-0.5)
    grad_score = (prob_full * (grad_prob - row_delta) * factor).astype(jnp.bfloat16)
    grad_query = jnp.einsum(
        "kgts,skd->tkgd", grad_score, key_list, preferred_element_type=jnp.float32
    ).astype(jnp.bfloat16)
    grad_key = jnp.einsum(
        "kgts,tkgd->skd", grad_score[..., cache_len:], queries, preferred_element_type=jnp.float32
    ).astype(jnp.bfloat16)
    grad_value = jnp.einsum(
        "kgts,tkgd->skd", prob_half[..., cache_len:], grad_heads, preferred_element_type=jnp.float32
    ).astype(jnp.bfloat16)
    return (grad_query, grad_key, grad_value)


def input_grad(in_rows, gain_row, grad_acts, grad_rows):
    parts = normalize(in_rows, gain_row)
    normed = parts[0]
    inverse = parts[1]
    grad_normed = grad_acts.astype(jnp.float32) * gain_row
    grad_input = inverse * (
        grad_normed - normed * jnp.mean(grad_normed * normed, axis=-1, keepdims=True)
    )
    return (grad_rows.astype(jnp.float32) + grad_input).astype(jnp.bfloat16)


def on_device(
    forward_in,
    backward_in,
    grad_out,
    cached_keys,
    cached_values,
    norm_gain,
    key_weight,
    value_weight,
    segment_index,
):
    ctx_size = lax.axis_size("ctx")
    rank_id = lax.axis_index("ctx")
    stretch_count = forward_in.shape[1]
    local_rows = forward_in.shape[2]
    model_width = forward_in.shape[3]
    kv_count = cached_keys.shape[3]
    head_size = cached_keys.shape[4]
    seg_len = local_rows * ctx_size
    cache_local = cached_keys.shape[2]
    cache_len = cache_local * ctx_size
    head_count = model_width // head_size
    group_size = head_count // kv_count
    local_heads = head_count // ctx_size
    kv_local = max(1, local_heads // group_size)
    copies = max(1, group_size // local_heads)
    sub_heads = local_heads // kv_local
    first_kv = rank_id * local_heads // group_size
    every_key, every_value = (
        lax.all_gather(cached_keys[0], "ctx", axis=1, tiled=True),
        lax.all_gather(cached_values[0], "ctx", axis=1, tiled=True),
    )
    head_keys = lax.dynamic_slice_in_dim(every_key, first_kv, kv_local, 2)
    head_values = lax.dynamic_slice_in_dim(every_value, first_kv, kv_local, 2)

    def as_queries(block):
        return block.reshape(seg_len, kv_local, sub_heads, head_size)

    def own_heads(block):
        return lax.dynamic_slice_in_dim(
            block.reshape(seg_len, kv_count, head_size), first_kv, kv_local, 1
        )

    forward_outs = []
    backward_outs = []
    for stretch in range(stretch_count):
        gain_row = norm_gain[0, stretch]
        key_rows = key_weight[0, stretch]
        value_rows = value_weight[0, stretch]
        forward_rows = forward_in[0, stretch]
        backward_rows = backward_in[0, stretch]
        grad_rows = grad_out[0, stretch]
        forward_acts = normalize(forward_rows, gain_row)[2]
        backward_acts = normalize(backward_rows, gain_row)[2]
        sent = (
            lax.all_to_all(
                forward_acts.reshape(local_rows, ctx_size, -1),
                "ctx",
                split_axis=1,
                concat_axis=0,
                tiled=True,
            ),
            lax.all_to_all(
                backward_acts.reshape(local_rows, ctx_size, -1),
                "ctx",
                split_axis=1,
                concat_axis=0,
                tiled=True,
            ),
            lax.all_to_all(
                grad_rows.reshape(local_rows, ctx_size, -1),
                "ctx",
                split_axis=1,
                concat_axis=0,
                tiled=True,
            ),
        )
        forward_slice = sent[0].reshape(seg_len, -1)
        backward_slice = sent[1].reshape(seg_len, -1)
        partial_value = jnp.stack(
            [
                jnp.dot(forward_slice, key_rows, preferred_element_type=jnp.float32),
                jnp.dot(forward_slice, value_rows, preferred_element_type=jnp.float32),
                jnp.dot(backward_slice, key_rows, preferred_element_type=jnp.float32),
                jnp.dot(backward_slice, value_rows, preferred_element_type=jnp.float32),
            ]
        )
        new_kv = lax.psum(partial_value.astype(jnp.bfloat16), "ctx")
        forward_key_list = jnp.concatenate([head_keys[stretch], own_heads(new_kv[0])], axis=0)
        forward_value_list = jnp.concatenate([head_values[stretch], own_heads(new_kv[1])], axis=0)
        backward_key_list = jnp.concatenate([head_keys[stretch], own_heads(new_kv[2])], axis=0)
        backward_value_list = jnp.concatenate([head_values[stretch], own_heads(new_kv[3])], axis=0)
        attended = attend(
            as_queries(forward_slice),
            forward_key_list,
            forward_value_list,
            segment_index[0, stretch, 0],
            cache_len,
        )[2]
        grad_query, grad_key, grad_value = attend_back(
            as_queries(backward_slice),
            backward_key_list,
            backward_value_list,
            segment_index[0, stretch, 1],
            cache_len,
            as_queries(sent[2]),
        )
        run_sums = jnp.stack([grad_key.reshape(seg_len, -1), grad_value.reshape(seg_len, -1)])
        every_run = lax.all_gather(run_sums, "ctx", axis=2, tiled=True)
        kv_grads = jnp.sum(
            every_run.reshape(2, seg_len, kv_count, copies, head_size).astype(jnp.float32), axis=3
        ).astype(jnp.bfloat16)
        kv_grads = kv_grads.reshape(2, seg_len, kv_count * head_size)
        back_rows = jnp.einsum(
            "te,de->td", kv_grads[0], key_rows, preferred_element_type=jnp.float32
        )
        back_rows = back_rows + jnp.einsum(
            "te,de->td", kv_grads[1], value_rows, preferred_element_type=jnp.float32
        )
        grad_acts = (grad_query.reshape(seg_len, -1).astype(jnp.float32) + back_rows).astype(
            jnp.bfloat16
        )
        returned = (
            lax.all_to_all(
                attended.reshape(ctx_size, local_rows, -1),
                "ctx",
                split_axis=0,
                concat_axis=2,
                tiled=True,
            ),
            lax.all_to_all(
                grad_acts.reshape(ctx_size, local_rows, -1),
                "ctx",
                split_axis=0,
                concat_axis=2,
                tiled=True,
            ),
        )
        attn_rows = returned[0].reshape(local_rows, model_width)
        section_out = (forward_rows.astype(jnp.float32) + attn_rows.astype(jnp.float32)).astype(
            jnp.bfloat16
        )
        section_grad = input_grad(
            backward_rows, gain_row, returned[1].reshape(local_rows, model_width), grad_rows
        )
        forward_outs.append(section_out)
        backward_outs.append(section_grad)
    pipe_rank = lax.axis_index("pipe")
    arrived = passed_along(jnp.stack(forward_outs), "pipe", 1)
    next_forward = jnp.where(pipe_rank == 0, jnp.roll(arrived, 1, axis=0), arrived)
    came_back = passed_along(jnp.stack(backward_outs), "pipe", -1)
    next_backward = jnp.where(
        pipe_rank == lax.axis_size("pipe") - 1, jnp.roll(came_back, -1, axis=0), came_back
    )
    return (next_forward[None], next_backward[None])


def solution(mesh):
    in_specs = (
        P("pipe", None, "ctx", None),
        P("pipe", None, "ctx", None),
        P("pipe", None, "ctx", None),
        P("pipe", None, "ctx", None, None),
        P("pipe", None, "ctx", None, None),
        P("pipe", None, None),
        P("pipe", None, "ctx", None),
        P("pipe", None, "ctx", None),
        P("pipe", None, None),
    )
    out_specs = (P("pipe", None, "ctx", None), P("pipe", None, "ctx", None))
    return jax.shard_map(
        on_device, mesh=mesh, in_specs=in_specs, out_specs=out_specs, check_vma=False
    )
```

profile of v0, /device:TPU:6, one launch (start us, length us, event | category | flops | bytes accessed | tf_op | source)
XLA Modules:
  0.0 993.1 jit_solution(6927345454423513771)
XLA Ops:
  38.2 34.3 %all-to-all-done.4 = bf16[128,4,2048]{0,2,1:T(8,128)(2,1)S(1)} async-done(((bf16[128,4,2048]{0,2,1:T(8,128)(2,1)}), bf16[128,4,2048]{0,2,1:T(8,128)(2,1)S(1)}, u32[]{:S(2)}, u32[]{:S(2)}) %all-to-all-start.4) | async-done | bytes 2097184 | tf_op jit(solution)/shard_map/all_to_all | solution.py:141
  93.9 8.9 all-to-all-done.3
  128.8 15.4 %all-to-all-done = bf16[128,4,2048]{0,2,1:T(8,128)(2,1)} async-done(((bf16[128,4,2048]{0,2,1:T(8,128)(2,1)}), bf16[128,4,2048]{0,2,1:T(8,128)(2,1)}, u32[]{:S(2)}, u32[]{:S(2)}) %all-to-all-start) | async-done | bytes 2097184 | tf_op jit(solution)/shard_map/all_to_all | solution.py:134
  164.9 9.5 all-to-all-done.1
  218.4 40.8 %all-to-all-done.8 = bf16[128,4,2048]{2,0,1:T(8,128)(2,1)} async-done(((bf16[128,4,2048]{2,0,1:T(8,128)(2,1)}), bf16[128,4,2048]{2,0,1:T(8,128)(2,1)}, u32[]{:S(2)}, u32[]{:S(2)}) %all-to-all-start.8) | async-done | bytes 2097184 | tf_op jit(solution)/shard_map/all_to_all | solution.py:148
  297.6 15.0 %all-to-all-done.6 = bf16[128,4,2048]{2,0,1:T(8,128)(2,1)} async-done(((bf16[128,4,2048]{2,0,1:T(8,128)(2,1)}), bf16[128,4,2048]{2,0,1:T(8,128)(2,1)}, u32[]{:S(2)}, u32[]{:S(2)}) %all-to-all-start.6) | async-done | bytes 2097184 | tf_op jit(solution)/shard_map/all_to_all | solution.py:148
  322.9 71.7 %all-reduce.3.cloned.1.call-done = (bf16[4,512,1024]{2,1,0:T(8,128)(2,1)}, bf16[4,512,1024]{2,1,0:T(8,128)(2,1)}) async-done(((bf16[4,512,1024]{2,1,0:T(8,128)(2,1)}, bf16[4,512,1024]{2,1,0:T(8,128)(2,1)}), (bf16[4,512,1024]{2,1,0:T(8,128)(2,1)}, bf16[4,512,1024]{2,1,0:T(8,128)(2,1)})) %all-reduce.3.cloned.1.call-update) | async-done | bytes 8388624 | tf_op jit(solution)/shard_map/psum | solution.py:166
  429.1 19.5 %fusion.279 = (f32[2,8,512]{2,1,0:T(8,128)S(1)}, f32[2,8,512,1024]{2,3,1,0:T(8,128)}) fusion(pred[512,1024]{0,1:T(8,128)(4,1)} %get-tuple-element.41, bf16[512,2,8,128]{3,2,1,0:T(8,128)(2,1)} %bitcast.526, bf16[512,2,128]{2,0,1:T(8,128)(2,1)S(1)} %get-tuple-element.30, bf16[512,2,128]{2,0,1:T(8,128)(2,1)} %copy.253), kind=kOutput, calls=%fused_computation.270 | convolution fusion | flops 2182087680 | bytes 36732928 | tf_op jit(solution)/shard_map/sub | solution.py:34
  448.6 13.2 %convert_bitcast_fusion.3 = bf16[512,2,8,128]{0,3,2,1:T(8,128)(2,1)} fusion(f32[2,8,512,1024]{2,3,1,0:T(8,128)} %get-tuple-element.49, f32[2,8,512]{2,1,0:T(8,128)S(1)} %get-tuple-element.48, bf16[512,2,128]{0,2,1:T(8,128)(2,1)S(1)} %get-tuple-element.28, bf16[512,2,128]{0,2,1:T(8,128)(2,1)S(1)} %constant_dynamic-slice_fusion.7), kind=kOutput, calls=%fused_computation.143 | convolution fusion | flops 2166358016 | bytes 36208640 | tf_op jit(solution)/shard_map/kgts,skd->tkgd/dot_general | solution.py:41
  474.7 17.2 %fusion.297 = (f32[2,8,512]{2,1,0:T(8,128)}, f32[2,8,512,1024]{2,3,1,0:T(8,128)}) fusion(pred[512,1024]{0,1:T(8,128)(4,1)} %get-tuple-element.38, bf16[512,2,8,128]{3,2,1,0:T(8,128)(2,1)} %bitcast.523, bf16[512,2,128]{2,0,1:T(8,128)(2,1)S(1)} %get-tuple-element.30, bf16[512,2,128]{2,0,1:T(8,128)(2,1)S(1)} %copy.258), kind=kOutput, calls=%fused_computation.272 | convolution fusion | flops 2182087680 | bytes 36732928 | tf_op jit(solution)/shard_map/sub | solution.py:34
  491.9 12.5 %fusion.28 = bf16[2,8,512,1024]{2,3,1,0:T(8,128)(2,1)S(1)} fusion(f32[2,8,512,1024]{2,3,1,0:T(8,128)} %get-tuple-element.53, f32[2,8,512]{2,1,0:T(8,128)} %get-tuple-element.52), kind=kLoop, calls=%fused_computation.42 | loop fusion | flops 16777216 | bytes 50364416 | tf_op jit(solution)/shard_map/convert_element_type | solution.py:40
  510.8 17.3 %fusion.9 = bf16[2,8,512,1024]{2,3,1,0:T(8,128)(2,1)} fusion(bf16[512,2,8,128]{0,3,2,1:T(8,128)(2,1)S(1)} %copy.188, f32[2,8,512]{2,1,0:T(8,128)} %bitcast.543, f32[2,8,512,1024]{2,3,1,0:T(8,128)} %get-tuple-element.53, f32[2,8,512]{2,1,0:T(8,128)} %get-tuple-element.52, bf16[512,2,128]{0,2,1:T(8,128)(2,1)S(1)} %get-tuple-element.28, ...), kind=kOutput, calls=%fused_computation.12 | convolution fusion | flops 2190475264 | bytes 53018624 | tf_op jit(solution)/shard_map/tkgd,skd->kgts/dot_general | solution.py:49
  535.5 14.9 %copy.192 = bf16[2,8,512,512]{3,1,0,2:T(8,128)(2,1)} copy(bf16[2,8,512,512]{2,3,1,0:T(8,128)(2,1)} %slice.188) | data formatting | bytes 16777216 | tf_op jit(solution)/shard_map/slice | solution.py:60
  557.0 17.3 %fusion.288 = (f32[2,8,512]{2,1,0:T(8,128)S(1)}, f32[2,8,512,1024]{2,3,1,0:T(8,128)}) fusion(pred[512,1024]{0,1:T(8,128)(4,1)S(1)} %copy-done.40, bf16[512,2,8,128]{3,2,1,0:T(8,128)(2,1)S(1)} %bitcast.522, bf16[512,2,128]{2,0,1:T(8,128)(2,1)S(1)} %copy-done.28, bf16[512,2,128]{2,0,1:T(8,128)(2,1)S(1)} %copy-done.33), kind=kOutput, calls=%fused_computation.271 | convolution fusion | flops 2182087680 | bytes 36732928 | tf_op jit(solution)/shard_map/sub | solution.py:34
  574.4 13.1 %fusion.29 = bf16[2,8,512,1024]{2,3,1,0:T(8,128)(2,1)S(1)} fusion(f32[2,8,512,1024]{2,3,1,0:T(8,128)} %get-tuple-element.51, f32[2,8,512]{2,1,0:T(8,128)S(1)} %get-tuple-element.50), kind=kLoop, calls=%fused_computation.43 | loop fusion | flops 16777216 | bytes 50364416 | tf_op jit(solution)/shard_map/convert_element_type | solution.py:40
  593.2 17.3 %fusion.6 = bf16[2,8,512,1024]{2,3,1,0:T(8,128)(2,1)} fusion(bf16[512,2,8,128]{0,3,2,1:T(8,128)(2,1)S(1)} %copy-done.14, f32[2,8,512]{2,1,0:T(8,128)S(1)} %bitcast.544, f32[2,8,512,1024]{2,3,1,0:T(8,128)} %get-tuple-element.51, f32[2,8,512]{2,1,0:T(8,128)S(1)} %get-tuple-element.50, bf16[512,2,128]{0,2,1:T(8,128)(2,1)S(1)} %copy-done.31, ...), kind=kOutput, calls=%fused_computation.7 | convolution fusion | flops 2190475264 | bytes 53018624 | tf_op jit(solution)/shard_map/tkgd,skd->kgts/dot_general | solution.py:49
  610.5 19.5 %fusion.270 = (f32[2,8,512]{2,1,0:T(8,128)S(1)}, f32[2,8,512,1024]{2,3,1,0:T(8,128)}) fusion(pred[512,1024]{0,1:T(8,128)(4,1)S(1)} %copy-done.39, bf16[512,2,8,128]{3,2,1,0:T(8,128)(2,1)} %bitcast.525, bf16[512,2,128]{2,0,1:T(8,128)(2,1)S(1)} %copy-done.28, bf16[512,2,128]{2,0,1:T(8,128)(2,1)} %copy.256), kind=kOutput, calls=%fused_computation.269 | convolution fusion | flops 2182087680 | bytes 36732928 | tf_op jit(solution)/shard_map/sub | solution.py:34
  630.1 13.5 %convert_bitcast_fusion.2 = bf16[512,2,8,128]{0,3,2,1:T(8,128)(2,1)} fusion(f32[2,8,512,1024]{2,3,1,0:T(8,128)} %get-tuple-element.47, f32[2,8,512]{2,1,0:T(8,128)S(1)} %get-tuple-element.46, bf16[512,2,128]{0,2,1:T(8,128)(2,1)S(1)} %copy-done.31, bf16[512,2,128]{0,2,1:T(8,128)(2,1)} %constant_dynamic-slice_fusion.5), kind=kOutput, calls=%fused_computation.142 | convolution fusion | flops 2166358016 | bytes 36208640 | tf_op jit(solution)/shard_map/kgts,skd->tkgd/dot_general | solution.py:41
  643.7 10.5 %convert_convert_fusion.1 = f32[2,128,8,512]{3,1,2,0:T(8,128)} fusion(bf16[2,8,512,1024]{2,3,1,0:T(8,128)(2,1)} %fusion.9, bf16[512,2,128]{2,0,1:T(8,128)(2,1)S(1)} %copy-done.30, bf16[512,2,128]{2,0,1:T(8,128)(2,1)S(1)} %copy-done.35), kind=kOutput, calls=%fused_computation.141 | convolution fusion | flops 2150629376 | bytes 21495808 | tf_op jit(solution)/shard_map/kgts,skd->tkgd/dot_general | solution.py:56
  660.1 7.4 slice.194
  680.2 14.9 %copy.211 = bf16[2,8,512,512]{3,1,0,2:T(8,128)(2,1)} copy(bf16[2,8,512,512]{2,3,1,0:T(8,128)(2,1)} %slice.194) | data formatting | bytes 16777216 | tf_op jit(solution)/shard_map/slice | solution.py:60
  721.7 31.4 %all-to-all-done.5 = bf16[4,128,2048]{1,2,0:T(8,128)(2,1)} async-done(((bf16[4,128,2048]{1,2,0:T(8,128)(2,1)}), bf16[4,128,2048]{1,2,0:T(8,128)(2,1)}, u32[]{:S(2)}, u32[]{:S(2)}) %all-to-all-start.5) | async-done | bytes 2097184 | tf_op jit(solution)/shard_map/all_to_all | solution.py:202
  818.8 8.5 all-to-all-done.9
  849.1 111.7 %collective-permute-done = bf16[2,128,8192]{1,2,0:T(8,128)(2,1)} collective-permute-done((bf16[2,128,8192]{1,2,0:T(8,128)(2,1)}, bf16[2,128,8192]{1,2,0:T(8,128)(2,1)}, u32[]{:S(2)}, u32[]{:S(2)}) %collective-permute-start) | collective-permute-done | bytes 4194336 | tf_op jit(solution)/shard_map/ppermute | solution.py:11
  (273 shorter events, 420.0 us)
Async XLA Ops:
  33.1 39.5 %all-to-all-start.4 = ((bf16[128,4,2048]{0,2,1:T(8,128)(2,1)}), bf16[128,4,2048]{0,2,1:T(8,128)(2,1)S(1)}, u32[]{:S(2)}, u32[]{:S(2)}) async-start(bf16[128,4,2048]{0,2,1:T(8,128)(2,1)} %get-tuple-element.36), calls=%async_computation.4 | async-start | bytes 4194304 | tf_op jit(solution)/shard_map/all_to_all | solution.py:141
  37.3 281.9 %all-gather.13.cloned.1.call-start = ((), (), s32[]{:S(2)}) async-start(), calls=%async_computation.13 | async-start | bytes 2621440 | tf_op jit(solution)/shard_map/all_gather | solution.py:108
  72.6 30.2 %all-to-all-start.3 = ((bf16[128,4,2048]{0,2,1:T(8,128)(2,1)}), bf16[128,4,2048]{0,2,1:T(8,128)(2,1)}, u32[]{:S(2)}, u32[]{:S(2)}) async-start(bf16[128,4,2048]{0,2,1:T(8,128)(2,1)} %get-tuple-element.37), calls=%async_computation.3 | async-start | bytes 4194304 | tf_op jit(solution)/shard_map/all_to_all | solution.py:134
  102.8 41.4 %all-to-all-start = ((bf16[128,4,2048]{0,2,1:T(8,128)(2,1)}), bf16[128,4,2048]{0,2,1:T(8,128)(2,1)}, u32[]{:S(2)}, u32[]{:S(2)}) async-start(bf16[128,4,2048]{0,2,1:T(8,128)(2,1)} %get-tuple-element.34), calls=%async_computation | async-start | bytes 4194304 | tf_op jit(solution)/shard_map/all_to_all | solution.py:134
  108.8 212.1 %all-gather.11.cloned.1.call-start = ((), (), s32[]{:S(2)}) async-start(), calls=%async_computation.12 | async-start | bytes 2621440 | tf_op jit(solution)/shard_map/all_gather | solution.py:109
  113.0 42.1 %copy-start.15 = (bf16[4,128,1,2048]{3,1,0,2:T(8,128)(2,1)}, bf16[4,128,1,2048]{3,1,0,2:T(8,128)(2,1)S(1)}, u32[]{:S(2)}) copy-start(bf16[4,128,1,2048]{3,1,0,2:T(8,128)(2,1)S(1)} %copy.172) | copy-start | bytes 6291460
  144.2 30.2 %all-to-all-start.1 = ((bf16[128,4,2048]{0,2,1:T(8,128)(2,1)}), bf16[128,4,2048]{0,2,1:T(8,128)(2,1)}, u32[]{:S(2)}, u32[]{:S(2)}) async-start(bf16[128,4,2048]{0,2,1:T(8,128)(2,1)} %get-tuple-element.35), calls=%async_computation.1 | async-start | bytes 4194304 | tf_op jit(solution)/shard_map/all_to_all | solution.py:141
  150.3 244.3 %all-reduce.3.cloned.1.call-start = ((), (), s32[]{:S(2)}) async-start(), calls=%async_computation.14 | async-start | bytes 16777216 | tf_op jit(solution)/shard_map/psum | solution.py:166
  164.9 26.0 %copy-start.18 = (bf16[4,128,1,2048]{3,1,0,2:T(8,128)(2,1)}, bf16[4,128,1,2048]{3,1,0,2:T(8,128)(2,1)S(1)}, u32[]{:S(2)}) copy-start(bf16[4,128,1,2048]{3,1,0,2:T(8,128)(2,1)S(1)} %copy.159) | copy-start | bytes 6291460
  206.5 52.7 %all-to-all-start.8 = ((bf16[128,4,2048]{2,0,1:T(8,128)(2,1)}), bf16[128,4,2048]{2,0,1:T(8,128)(2,1)}, u32[]{:S(2)}, u32[]{:S(2)}) async-start(bf16[128,4,2048]{2,0,1:T(8,128)(2,1)} %copy.204), calls=%async_computation.8 | async-start | bytes 4194304 | tf_op jit(solution)/shard_map/all_to_all | solution.py:148
  215.7 43.5 %copy-start.13 = (bf16[1,1,128,8192]{2,3,1,0:T(8,128)(2,1)}, bf16[1,1,128,8192]{2,3,1,0:T(8,128)(2,1)S(1)}, u32[]{:S(2)}) copy-start(bf16[1,1,128,8192]{2,3,1,0:T(8,128)(2,1)S(1)} %copy.257) | copy-start | bytes 6291460
  215.7 50.2 %copy-start.53 = (s32[1,2,2]{2,1,0:T(2,128)S(1)}, s32[1,2,2]{2,1,0:T(2,128)}, u32[]{:S(2)}) copy-start(s32[1,2,2]{2,1,0:T(2,128)} %param.17) | copy-start | bytes 52
  259.2 53.4 %all-to-all-start.6 = ((bf16[128,4,2048]{2,0,1:T(8,128)(2,1)}), bf16[128,4,2048]{2,0,1:T(8,128)(2,1)}, u32[]{:S(2)}, u32[]{:S(2)}) async-start(bf16[128,4,2048]{2,0,1:T(8,128)(2,1)} %copy.185), calls=%async_computation.6 | async-start | bytes 4194304 | tf_op jit(solution)/shard_map/all_to_all | solution.py:148
  321.0 153.7 %copy-start.29 = (bf16[512,2,128]{2,0,1:T(8,128)(2,1)}, bf16[512,2,128]{2,0,1:T(8,128)(2,1)S(1)}, u32[]{:S(2)}) copy-start(bf16[512,2,128]{2,0,1:T(8,128)(2,1)S(1)} %get-tuple-element.30) | copy-start | bytes 786436
  424.6 50.1 %copy-start.34 = (bf16[512,2,128]{2,0,1:T(8,128)(2,1)}, bf16[512,2,128]{2,0,1:T(8,128)(2,1)S(1)}, u32[]{:S(2)}) copy-start(bf16[512,2,128]{2,0,1:T(8,128)(2,1)S(1)} %copy.258) | copy-start | bytes 786436
  468.9 244.0 %all-to-all-start.2 = ((bf16[4,128,2048]{1,2,0:T(8,128)(2,1)}), bf16[4,128,2048]{1,2,0:T(8,128)(2,1)}, u32[]{:S(2)}, u32[]{:S(2)}) async-start(bf16[4,128,2048]{1,2,0:T(8,128)(2,1)} %copy.168), calls=%async_computation.2 | async-start | bytes 4194304 | tf_op jit(solution)/shard_map/all_to_all | solution.py:202
  474.7 282.2 %all-gather.7.cloned.1.call-start = ((), (), s32[]{:S(2)}) async-start(), calls=%async_computation.10 | async-start | bytes 2621440 | tf_op jit(solution)/shard_map/all_gather | solution.py:187
  556.9 222.5 %all-gather.9.cloned.1.call-start = ((), (), s32[]{:S(2)}) async-start(), calls=%async_computation.11 | async-start | bytes 2621440 | tf_op jit(solution)/shard_map/all_gather | solution.py:187
  713.0 40.2 %all-to-all-start.5 = ((bf16[4,128,2048]{1,2,0:T(8,128)(2,1)}), bf16[4,128,2048]{1,2,0:T(8,128)(2,1)}, u32[]{:S(2)}, u32[]{:S(2)}) async-start(bf16[4,128,2048]{1,2,0:T(8,128)(2,1)} %copy.179), calls=%async_computation.5 | async-start | bytes 4194304 | tf_op jit(solution)/shard_map/all_to_all | solution.py:202
  721.7 33.3 %copy-start.8 = (bf16[1,1,128,8192]{2,3,1,0:T(8,128)(2,1)S(1)}, bf16[1,1,128,8192]{2,3,1,0:T(8,128)(2,1)}, u32[]{:S(2)}) copy-start(bf16[1,1,128,8192]{2,3,1,0:T(8,128)(2,1)} %copy-done.7) | copy-start | bytes 6291460
  767.8 29.3 %all-to-all-start.7 = ((bf16[4,128,2048]{2,1,0:T(8,128)(2,1)}), bf16[4,128,2048]{2,1,0:T(8,128)(2,1)S(1)}, u32[]{:S(2)}, u32[]{:S(2)}) async-start(bf16[4,128,2048]{2,1,0:T(8,128)(2,1)} %bitcast.528), calls=%async_computation.7 | async-start | bytes 4194304 | tf_op jit(solution)/shard_map/all_to_all | solution.py:209
  777.7 183.1 %collective-permute-start = (bf16[2,128,8192]{1,2,0:T(8,128)(2,1)}, bf16[2,128,8192]{1,2,0:T(8,128)(2,1)}, u32[]{:S(2)}, u32[]{:S(2)}) collective-permute-start(bf16[2,128,8192]{1,2,0:T(8,128)(2,1)} %pad_maximum_fusion.2), channel_id=1, source_target_pairs={{0,4},{4,8},{8,12},{12,16},{16,20},{20,24},{24,28},{28,0},{1,5},{5... | collective-permute-start | bytes 12582920 | tf_op jit(solution)/shard_map/ppermute | solution.py:11
  797.1 30.2 %all-to-all-start.9 = ((bf16[4,128,2048]{2,1,0:T(8,128)(2,1)}), bf16[4,128,2048]{2,1,0:T(8,128)(2,1)}, u32[]{:S(2)}, u32[]{:S(2)}) async-start(bf16[4,128,2048]{2,1,0:T(8,128)(2,1)} %bitcast.527), calls=%async_computation.9 | async-start | bytes 4194304 | tf_op jit(solution)/shard_map/all_to_all | solution.py:209
  848.5 125.0 %collective-permute-start.1 = (bf16[2,128,8192]{1,2,0:T(8,128)(2,1)}, bf16[2,128,8192]{1,2,0:T(8,128)(2,1)}, u32[]{:S(2)}, u32[]{:S(2)}) collective-permute-start(bf16[2,128,8192]{1,2,0:T(8,128)(2,1)} %pad_maximum_fusion.3), channel_id=1, source_target_pairs={{0,28},{4,0},{8,4},{12,8},{16,12},{20,16},{24,20},{28,24},{1,29},{... | collective-permute-start | bytes 12582920 | tf_op jit(solution)/shard_map/ppermute | solution.py:11
  (53 other events, 354.6 us)
Sparse Core Ops, SparseCore 0:
  39.7 34.1 all-gather.12
  111.2 34.4 all-gather.10
  195.8 198.7 all-reduce.2
  557.1 22.5 all-gather.6
  713.1 33.9 all-gather.8
where the time goes:
time: 1010 us; the launch traced here: 993 us
  waiting for transfers between devices  354 us (35%)
  local copies, waits for them, and re-layouts  235 us (23%)
  matrix products  233 us (23%)
  other arithmetic  94.4 us (9%)
  starting transfers between devices  59.4 us (6%)
  between operations  17.7 us (2%)
    ppermute x2, waiting for transfers between devices, passed_along(): lax.ppermute(array, axis, [(i, (i + by) % count) for i in range(count)])  112 us
    sub x4, matrix products, probabilities(): lifted = jnp.exp(scores - row_max)  73.5 us
    psum x1, waiting for transfers between devices, on_device(): new_kv = lax.psum(partial_value.astype(jnp.bfloat16), 'ctx')  71.7 us
    unnamed x142, local copies, waits for them, and re-layouts  62.9 us
    all_to_all x2, waiting for transfers between devices, on_device(): lax.all_to_all(grad_rows.reshape(local_rows, ctx_size, -1), 'ctx', split_...  55.8 us
    slice x4, local copies, waits for them, and re-layouts, attend_back(): grad_score[..., cache_len:]  44.7 us
    all_to_all x2, waiting for transfers between devices, on_device(): lax.all_to_all(backward_acts.reshape(local_rows, ctx_size, -1), 'ctx', sp...  43.9 us
    dot_general x2, matrix products, attend_back(): jnp.einsum('tkgd,skd->kgts', grad_heads, value_list, preferred_element_ty...  34.7 us
  transfers between devices with their start and end apart: 17, of which 11 were waited for; matrix products, arithmetic and copies ran while one was open for 44% of the time, Pallas kernels for 0%

commit v1 on v0

v1 whole, which is shorter than its diff:
```python
import functools

import jax
import jax.numpy as jnp
from jax import lax
from jax.experimental import pallas as pl
from jax.experimental.pallas import tpu as pltpu
from jax.sharding import PartitionSpec as P

NEGATIVE = -1e30
LOG2_E = 1.4426950408889634
EPSILON = 1e-05
VMEM_LIMIT = 50 * 1024 * 1024


def call(kernel, grid, in_specs, out_specs, out_shape, scratch=(), flops=0, moved=0, name=None):
    return pl.pallas_call(
        kernel,
        grid=grid,
        in_specs=in_specs,
        out_specs=out_specs,
        out_shape=out_shape,
        scratch_shapes=list(scratch),
        compiler_params=pltpu.CompilerParams(
            vmem_limit_bytes=VMEM_LIMIT,
            dimension_semantics=("arbitrary",) * len(grid),
        ),
        cost_estimate=pl.CostEstimate(flops=int(flops), bytes_accessed=int(moved), transcendentals=0),
        name=name,
    )


def half(shape):
    return jax.ShapeDtypeStruct(shape, jnp.bfloat16)


def nt_dot(a, b):
    return lax.dot_general(a, b, (((1,), (1,)), ((), ())), preferred_element_type=jnp.float32)


def tn_dot(a, b):
    return lax.dot_general(a, b, (((0,), (0,)), ((), ())), preferred_element_type=jnp.float32)


def nn_dot(a, b):
    return jnp.dot(a, b, preferred_element_type=jnp.float32)


def norm_kernel(stretch, count, width, has_grad, *refs):
    rows_ref, gain_ref = refs[0], refs[1]
    acts_ref = refs[-2] if has_grad else refs[-1]
    rows = rows_ref[0, 0].astype(jnp.float32)
    inverse = lax.rsqrt(jnp.mean(rows * rows, axis=-1, keepdims=True) + EPSILON)
    acts = (rows * inverse * gain_ref[0, stretch : stretch + 1, :]).astype(jnp.bfloat16)
    for r in range(count):
        acts_ref[r] = acts[:, r * width : (r + 1) * width]
        if has_grad:
            refs[-1][r] = refs[2][0, 0, :, r * width : (r + 1) * width]


def norm_rows(rows, gain, stretch, count, grad=None):
    local_rows, model = rows.shape[2], rows.shape[3]
    width = model // count
    step = min(32, local_rows)
    row_spec = pl.BlockSpec((1, 1, step, model), lambda i: (0, stretch, i, 0))
    out_spec = pl.BlockSpec((count, step, width), lambda i: (0, i, 0))
    shape = half((count, local_rows, width))
    has_grad = grad is not None
    return call(
        functools.partial(norm_kernel, stretch, count, width, has_grad),
        (local_rows // step,),
        [row_spec, pl.BlockSpec(gain.shape, lambda i: (0, 0, 0))] + [row_spec] * has_grad,
        (out_spec, out_spec) if has_grad else out_spec,
        (shape, shape) if has_grad else shape,
        flops=6 * local_rows * model,
        moved=4 * local_rows * model * (1 + has_grad),
        name="norm_rows",
    )(*((rows, gain) + ((grad,) if has_grad else ())))


def project_kernel(kv_width, acts_ref, key_ref, value_ref, out_ref):
    acts = acts_ref[...]
    out_ref[0, :, :kv_width] = nn_dot(acts, key_ref[0, 0]).astype(jnp.bfloat16)
    out_ref[0, :, kv_width:] = nn_dot(acts, value_ref[0, 0]).astype(jnp.bfloat16)


def project(acts, key_weight, value_weight, stretch, count, kv_width, copies):
    tokens, width = acts.shape
    weight_spec = pl.BlockSpec((1, 1, width, kv_width), lambda r: (0, stretch, 0, r // copies))
    return call(
        functools.partial(project_kernel, kv_width),
        (count,),
        [pl.BlockSpec((tokens, width), lambda r: (0, 0)), weight_spec, weight_spec],
        pl.BlockSpec((1, tokens, 2 * kv_width), lambda r: (r, 0, 0)),
        half((count, tokens, 2 * kv_width)),
        flops=4 * tokens * width * kv_width * count,
        moved=2 * (tokens * width + 2 * width * kv_width * count + 2 * tokens * kv_width * count),
        name="project_kv",
    )(acts, key_weight, value_weight)


def load_lists(count, new_key, new_value, old_key, old_value, keys, values, own_keys, own_values):
    for new, old, kept, own in (
        (new_key, old_key, keys, own_keys),
        (new_value, old_value, values, own_values),
    ):
        total = new[0].astype(jnp.float32)
        for r in range(1, count):
            total = total + new[r].astype(jnp.float32)
        own[...] = total.astype(jnp.bfloat16)
        cached = old[:, 0, 0]
        kept[...] = cached.reshape(kept.shape)


def score_pieces(queries, start, rows, cached, keys, own_keys):
    pieces = []
    if cached:
        pieces.append(nt_dot(queries, keys[...]))
    if start:
        pieces.append(nt_dot(queries, own_keys[:start]))
    diagonal = nt_dot(queries, own_keys[start : start + rows])
    column = lax.broadcasted_iota(jnp.int32, (rows, rows), 1)
    row_ids = lax.broadcasted_iota(jnp.int32, (rows, rows), 0)
    pieces.append(jnp.where(column <= row_ids, diagonal, NEGATIVE))
    return pieces


def lifted_pieces(pieces, scale):
    row_max = pieces[0].max(axis=-1, keepdims=True)
    for piece in pieces[1:]:
        row_max = jnp.maximum(row_max, piece.max(axis=-1, keepdims=True))
    lifted = [jnp.exp2((piece - row_max) * scale) for piece in pieces]
    total = lifted[0].sum(axis=-1, keepdims=True)
    for piece in lifted[1:]:
        total = total + piece.sum(axis=-1, keepdims=True)
    return lifted, 1.0 / total


def list_pieces(start, rows, cached, kept, own):
    pieces = [kept[...]] if cached else []
    if start:
        pieces.append(own[:start])
    pieces.append(own[start : start + rows])
    return pieces


def sum_of(terms):
    total = terms[0]
    for term in terms[1:]:
        total = total + term
    return total


def attend_kernel(
    count, head, rows, per_step, place, segment, q_ref, nk, nv, ok, ov, out_ref, keys, values, own_keys, own_values
):
    @pl.when(pl.program_id(1) == 0)
    def _():
        load_lists(count, nk, nv, ok, ov, keys, values, own_keys, own_values)

    scale = head**-0.5 * LOG2_E
    tokens = q_ref.shape[0]

    def work(cached):
        for h in range(per_step):
            cols = slice(h * head, (h + 1) * head)
            for start in range(0, tokens, rows):
                part = slice(start, start + rows)
                queries = q_ref[part, cols]
                lifted, inverse = lifted_pieces(
                    score_pieces(queries, start, rows, cached, keys, own_keys), scale
                )
                value_pieces = list_pieces(start, rows, cached, values, own_values)
                attended = sum_of(
                    [nn_dot(e.astype(jnp.bfloat16), v) for e, v in zip(lifted, value_pieces)]
                )
                out_ref[part, cols] = (attended * inverse).astype(jnp.bfloat16)

    visible = segment[0, place[0], place[1]] > 0
    pl.when(visible)(lambda: work(True))
    pl.when(jnp.logical_not(visible))(lambda: work(False))


def attend_back_kernel(
    count, head, rows, per_step, place, segment, q_ref, g_ref, nk, nv, ok, ov,
    dq_ref, kv_ref, keys, values, own_keys, own_values, key_sum, value_sum
):
    @pl.when(pl.program_id(1) == 0)
    def _():
        load_lists(count, nk, nv, ok, ov, keys, values, own_keys, own_values)
        key_sum[...] = jnp.zeros_like(key_sum)
        value_sum[...] = jnp.zeros_like(value_sum)

    factor = head**-0.5
    tokens = q_ref.shape[0]

    def work(cached):
        for h in range(per_step):
            cols = slice(h * head, (h + 1) * head)
            for start in range(0, tokens, rows):
                part = slice(start, start + rows)
                queries = q_ref[part, cols]
                grads = g_ref[part, cols]
                lifted, inverse = lifted_pieces(
                    score_pieces(queries, start, rows, cached, keys, own_keys), factor * LOG2_E
                )
                value_pieces = list_pieces(start, rows, cached, values, own_values)
                key_pieces = list_pieces(start, rows, cached, keys, own_keys)
                rounded = [e.astype(jnp.bfloat16) for e in lifted]
                attended = sum_of([nn_dot(e, v) for e, v in zip(rounded, value_pieces)]) * inverse
                wide = grads.astype(jnp.float32)
                delta = jnp.sum(wide * attended, axis=-1, keepdims=True)
                scores = [
                    (e * (nt_dot(grads, v) - delta)).astype(jnp.bfloat16)
                    for e, v in zip(lifted, value_pieces)
                ]
                row_scale = inverse * factor
                dq = sum_of([nn_dot(s, k) for s, k in zip(scores, key_pieces)]) * row_scale
                dq_ref[part, cols] = dq.astype(jnp.bfloat16)
                scaled_q = (queries.astype(jnp.float32) * row_scale).astype(jnp.bfloat16)
                scaled_g = (wide * inverse).astype(jnp.bfloat16)
                if start:
                    key_sum[:start] += tn_dot(scores[-2], scaled_q)
                    value_sum[:start] += tn_dot(rounded[-2], scaled_g)
                key_sum[part] += tn_dot(scores[-1], scaled_q)
                value_sum[part] += tn_dot(rounded[-1], scaled_g)

    visible = segment[0, place[0], place[1]] > 0
    pl.when(visible)(lambda: work(True))
    pl.when(jnp.logical_not(visible))(lambda: work(False))

    @pl.when(pl.program_id(1) == pl.num_programs(1) - 1)
    def _():
        kv_ref[0] = key_sum[...].astype(jnp.bfloat16)
        kv_ref[1] = value_sum[...].astype(jnp.bfloat16)


def attention(segment, place, queries, new_kv, cache, kv_local, head, grads=None):
    tokens, width = queries.shape
    count, cache_local = cache.shape[0], cache.shape[3]
    cache_len = count * cache_local
    sub_heads = width // head // kv_local
    per_step = 2 if sub_heads % 2 == 0 else 1
    steps = sub_heads // per_step
    rows = min(256, tokens)
    stretch = place[0]
    head_spec = pl.BlockSpec((tokens, per_step * head), lambda j, g: (0, j * steps + g))
    in_specs = [pl.BlockSpec(memory_space=pltpu.SMEM), head_spec] + [head_spec] * (grads is not None)
    in_specs += [
        pl.BlockSpec((count, tokens, head), lambda j, g: (0, 0, j)),
        pl.BlockSpec((count, tokens, head), lambda j, g: (0, 0, kv_local + j)),
        pl.BlockSpec((count, 1, 1, cache_local, head), lambda j, g: (0, 0, stretch, 0, j)),
        pl.BlockSpec((count, 1, 1, cache_local, head), lambda j, g: (0, 1, stretch, 0, j)),
    ]
    scratch = [pltpu.VMEM((cache_len, head), jnp.bfloat16)] * 2
    scratch += [pltpu.VMEM((tokens, head), jnp.bfloat16)] * 2
    tail = (new_kv, new_kv, cache, cache)
    unit = 2 * tokens * width * (cache_len + tokens)
    if grads is None:
        return call(
            functools.partial(attend_kernel, count, head, rows, per_step, place),
            (kv_local, steps),
            in_specs,
            head_spec,
            half((tokens, width)),
            scratch,
            flops=2 * unit,
            moved=4 * tokens * width,
            name="attend",
        )(segment, queries, *tail)
    return call(
        functools.partial(attend_back_kernel, count, head, rows, per_step, place),
        (kv_local, steps),
        in_specs,
        (head_spec, pl.BlockSpec((2, tokens, head), lambda j, g: (0, 0, j))),
        (half((tokens, width)), half((2, tokens, kv_local * head))),
        scratch + [pltpu.VMEM((tokens, head), jnp.float32)] * 2,
        flops=5 * unit,
        moved=8 * tokens * width,
        name="attend_back",
    )(segment, queries, grads, *tail)


def back_kernel(count, copies, dq_ref, every_ref, key_ref, value_ref, out_ref, totals):
    kv_width = every_ref.shape[3]

    @pl.when(pl.program_id(0) == 0)
    def _():
        for which in range(2):
            for j in range(count // copies):
                total = every_ref[j * copies, which].astype(jnp.float32)
                for extra in range(1, copies):
                    total = total + every_ref[j * copies + extra, which].astype(jnp.float32)
                totals[which, :, j * kv_width : (j + 1) * kv_width] = total.astype(jnp.bfloat16)

    back = nt_dot(totals[0], key_ref[0, 0]) + nt_dot(totals[1], value_ref[0, 0])
    out_ref[...] = (dq_ref[...].astype(jnp.float32) + back).astype(jnp.bfloat16)


def back_rows(dq, every, key_weight, value_weight, stretch, copies):
    tokens, width = dq.shape
    count = every.shape[0]
    kv_total = key_weight.shape[3]
    step = min(512, width)
    weight_spec = pl.BlockSpec((1, 1, step, kv_total), lambda n: (0, stretch, n, 0))
    tile_spec = pl.BlockSpec((tokens, step), lambda n: (0, n))
    return call(
        functools.partial(back_kernel, count, copies),
        (width // step,),
        [tile_spec, pl.BlockSpec(every.shape, lambda n: (0, 0, 0, 0)), weight_spec, weight_spec],
        tile_spec,
        half((tokens, width)),
        [pltpu.VMEM((2, tokens, kv_total), jnp.bfloat16)],
        flops=4 * tokens * width * kv_total,
        moved=4 * tokens * width + 4 * width * kv_total,
        name="back_rows",
    )(dq, every, key_weight, value_weight)


def add_kernel(count, width, rows_ref, attn_ref, out_ref):
    for r in range(count):
        cols = slice(r * width, (r + 1) * width)
        out_ref[:, cols] = (
            rows_ref[0, 0, :, cols].astype(jnp.float32) + attn_ref[r].astype(jnp.float32)
        ).astype(jnp.bfloat16)


def add_rows(rows, attn, stretch):
    local_rows, model = rows.shape[2], rows.shape[3]
    count, width = attn.shape[0], attn.shape[2]
    step = min(32, local_rows)
    return call(
        functools.partial(add_kernel, count, width),
        (local_rows // step,),
        [
            pl.BlockSpec((1, 1, step, model), lambda i: (0, stretch, i, 0)),
            pl.BlockSpec((count, step, width), lambda i: (0, i, 0)),
        ],
        pl.BlockSpec((step, model), lambda i: (i, 0)),
        half((local_rows, model)),
        flops=2 * local_rows * model,
        moved=6 * local_rows * model,
        name="add_rows",
    )(rows, attn)


def grad_kernel(stretch, count, width, rows_ref, gain_ref, acts_ref, grad_ref, out_ref):
    rows = rows_ref[0, 0].astype(jnp.float32)
    inverse = lax.rsqrt(jnp.mean(rows * rows, axis=-1, keepdims=True) + EPSILON)
    inner = jnp.zeros_like(inverse)
    for r in range(count):
        cols = slice(r * width, (r + 1) * width)
        grad_normed = acts_ref[r].astype(jnp.float32) * gain_ref[0, stretch : stretch + 1, cols]
        inner = inner + jnp.sum(grad_normed * (rows[:, cols] * inverse), axis=-1, keepdims=True)
    mean = inner / (count * width)
    for r in range(count):
        cols = slice(r * width, (r + 1) * width)
        grad_normed = acts_ref[r].astype(jnp.float32) * gain_ref[0, stretch : stretch + 1, cols]
        grad_input = inverse * (grad_normed - rows[:, cols] * inverse * mean)
        out_ref[:, cols] = (grad_ref[0, 0, :, cols].astype(jnp.float32) + grad_input).astype(
            jnp.bfloat16
        )


def grad_rows(rows, gain, acts, grads, stretch):
    local_rows, model = rows.shape[2], rows.shape[3]
    count, width = acts.shape[0], acts.shape[2]
    step = min(32, local_rows)
    row_spec = pl.BlockSpec((1, 1, step, model), lambda i: (0, stretch, i, 0))
    return call(
        functools.partial(grad_kernel, stretch, count, width),
        (local_rows // step,),
        [
            row_spec,
            pl.BlockSpec(gain.shape, lambda i: (0, 0, 0)),
            pl.BlockSpec((count, step, width), lambda i: (0, i, 0)),
            row_spec,
        ],
        pl.BlockSpec((step, model), lambda i: (i, 0)),
        half((local_rows, model)),
        flops=10 * local_rows * model,
        moved=8 * local_rows * model,
        name="grad_rows",
    )(rows, gain, acts, grads)


def place_shifted(by, count, swap_ref, *refs):
    out_ref = refs[-1]
    swap = swap_ref[0] > 0

    @pl.when(swap)
    def _():
        for s in range(count):
            out_ref[0, (s + by) % count] = refs[s][...]

    @pl.when(jnp.logical_not(swap))
    def _():
        for s in range(count):
            out_ref[0, s] = refs[s][...]


def place_rows(arrived, swap, by):
    local_rows, model = arrived[0].shape
    count = len(arrived)
    step = min(32, local_rows)
    return call(
        functools.partial(place_shifted, by, count),
        (local_rows // step,),
        [pl.BlockSpec(memory_space=pltpu.SMEM)]
        + [pl.BlockSpec((step, model), lambda i: (i, 0))] * count,
        pl.BlockSpec((1, count, step, model), lambda i: (0, 0, i, 0)),
        half((1, count, local_rows, model)),
        moved=4 * count * local_rows * model,
        name="place_rows",
    )(swap.astype(jnp.int32).reshape(1), *arrived)


def passed_along(array, axis, by):
    count = lax.axis_size(axis)
    return lax.ppermute(array, axis, [(i, (i + by) % count) for i in range(count)])


def exchange(blocks):
    return lax.all_to_all(blocks, "ctx", split_axis=0, concat_axis=0, tiled=True)


def on_device(
    forward_in,
    backward_in,
    grad_out,
    cached_keys,
    cached_values,
    norm_gain,
    key_weight,
    value_weight,
    segment_index,
):
    count = lax.axis_size("ctx")
    stretch_count, local_rows, model = forward_in.shape[1:]
    cache_local, kv_count, head = cached_keys.shape[2:]
    tokens = local_rows * count
    width = model // count
    group_size = model // head // kv_count
    local_heads = model // head // count
    kv_local = max(1, local_heads // group_size)
    copies = max(1, group_size // local_heads)
    kv_width = kv_local * head
    assert cache_local * count <= tokens

    stretches = range(stretch_count)

    def flat(blocks):
        return blocks.reshape(tokens, width)

    def split(block):
        return block.reshape(count, local_rows, width)

    both = jnp.stack([cached_keys[0], cached_values[0]])
    both = both.reshape(2, stretch_count, cache_local, kv_count * head)
    cache_sent = jnp.stack(
        [both[..., (r // copies) * kv_width : (r // copies + 1) * kv_width] for r in range(count)]
    )

    forward, backward, grads, forward_kv, backward_kv = {}, {}, {}, {}, {}
    for s in stretches:
        forward_acts = norm_rows(forward_in, norm_gain, s, count)
        backward_acts, grad_blocks = norm_rows(backward_in, norm_gain, s, count, grad_out)
        forward[s] = flat(exchange(forward_acts))
        backward[s] = flat(exchange(backward_acts))
        grads[s] = flat(exchange(grad_blocks))
    cache = exchange(cache_sent)
    for s in stretches:
        weights = (key_weight, value_weight, s, count, kv_width, copies)
        forward_kv[s] = exchange(project(forward[s], *weights))
        backward_kv[s] = exchange(project(backward[s], *weights))
    arrived, came_back = [], []
    for s in stretches:
        attended = attention(
            segment_index, (s, 0), forward[s], forward_kv[s], cache, kv_local, head
        )
        section_out = add_rows(forward_in, exchange(split(attended)), s)
        arrived.append(passed_along(section_out, "pipe", 1))
        dq, run_sums = attention(
            segment_index, (s, 1), backward[s], backward_kv[s], cache, kv_local, head, grads[s]
        )
        every = lax.all_gather(run_sums, "ctx", axis=0, tiled=False)
        grad_acts = back_rows(dq, every, key_weight, value_weight, s, copies)
        section_grad = grad_rows(backward_in, norm_gain, exchange(split(grad_acts)), grad_out, s)
        came_back.append(passed_along(section_grad, "pipe", -1))
    rank = lax.axis_index("pipe")
    next_forward = place_rows(arrived, rank == 0, 1)
    next_backward = place_rows(came_back, rank == lax.axis_size("pipe") - 1, -1)
    return (next_forward, next_backward)


def solution(mesh):
    in_specs = (
        P("pipe", None, "ctx", None),
        P("pipe", None, "ctx", None),
        P("pipe", None, "ctx", None),
        P("pipe", None, "ctx", None, None),
        P("pipe", None, "ctx", None, None),
        P("pipe", None, None),
        P("pipe", None, "ctx", None),
        P("pipe", None, "ctx", None),
        P("pipe", None, None),
    )
    out_specs = (P("pipe", None, "ctx", None), P("pipe", None, "ctx", None))
    return jax.shard_map(
        on_device, mesh=mesh, in_specs=in_specs, out_specs=out_specs, check_vma=False
    )
```

time: 1010 us -> 683 us (0.68); the launches traced: 993 us -> 679 us
  matrix products: 233 us -> 0 us
  local copies, waits for them, and re-layouts: 235 us -> 8.75 us
  Pallas kernels: 0 us -> 201 us
  other arithmetic: 94.4 us -> 2.4 us
  blocking collectives: 0 us -> 57.8 us
  waiting for transfers between devices: 354 us -> 321 us
  starting transfers between devices: 59.4 us -> 74.3 us
    pallas_call x0 -> x20, Pallas kernels: none -> 201 us  [the longest x2 60.8 us: attention(): call(functools.partial(attend_back_kernel, count, head, rows, per_step, p...]
    dot_general x24 -> x0, matrix products: 159 us -> none  [the longest x2 34.7 us: attend_back(): jnp.einsum('tkgd,skd->kgts', grad_heads, value_list, preferred_element_ty...]
    slice x17 -> x0, local copies, waits for them, and re-layouts: 83 us -> none  [the longest x4 44.7 us: attend_back(): grad_score[..., cache_len:]]
    sub x4 -> x0, matrix products: 73.5 us -> none  [probabilities(): lifted = jnp.exp(scores - row_max)]
    psum x1 -> x0, waiting for transfers between devices: 71.7 us -> none  [on_device(): new_kv = lax.psum(partial_value.astype(jnp.bfloat16), 'ctx')]
    convert_element_type x14 -> x0, other arithmetic: 59.2 us -> none  [the longest x2 25.6 us: attend(): prob_half = prob_full.astype(jnp.bfloat16)]
    all_to_all x0 -> x2, blocking collectives: none -> 57.8 us  [exchange(): lax.all_to_all(blocks, 'ctx', split_axis=0, concat_axis=0, tiled=True)]
    unnamed x142 -> x16, local copies, waits for them, and re-layouts: 62.9 us -> 8.16 us
  transfers between devices with their start and end apart: 17 -> 19, of which waited for: 11 -> 13; matrix products, arithmetic and copies ran while one was open for 44% -> 0% of each run, Pallas kernels for 0% -> 29%
where the time goes in v1:
time: 683 us; the launch traced here: 679 us
  waiting for transfers between devices  321 us (47%)
  Pallas kernels  201 us (29%)
  starting transfers between devices  74.3 us (11%)
  blocking collectives  57.8 us (8%)
  between operations  14.1 us (2%)
  local copies, waits for them, and re-layouts  8.75 us (1%)
    all_to_all x13, waiting for transfers between devices, exchange(): lax.all_to_all(blocks, 'ctx', split_axis=0, concat_axis=0, tiled=True)  165 us
    ppermute x4, waiting for transfers between devices, passed_along(): lax.ppermute(array, axis, [(i, (i + by) % count) for i in range(count)])  156 us
    all_to_all x13, starting transfers between devices, exchange(): lax.all_to_all(blocks, 'ctx', split_axis=0, concat_axis=0, tiled=True)  71.2 us
    pallas_call x2, Pallas kernels, attention(): call(functools.partial(attend_back_kernel, count, head, rows, per_step, p...  60.8 us
    all_to_all x2, blocking collectives, exchange(): lax.all_to_all(blocks, 'ctx', split_axis=0, concat_axis=0, tiled=True)  57.8 us
    pallas_call x2, Pallas kernels, attention(): call(functools.partial(attend_kernel, count, head, rows, per_step, place)...  38.8 us
    pallas_call x4, Pallas kernels, project(): call(functools.partial(project_kernel, kv_width), (count,), [pl.BlockSpec...  34.9 us
    pallas_call x2, Pallas kernels, back_rows(): call(functools.partial(back_kernel, count, copies), (width // step,), [ti...  19.5 us
  transfers between devices with their start and end apart: 19, of which 13 were waited for; matrix products, arithmetic and copies ran while one was open for 0% of the time, Pallas kernels for 29%

profile of v1, /device:TPU:6, one launch (start us, length us, event | category | flops | bytes accessed | tf_op | source)
XLA Modules:
  0.0 679.2 jit_solution(3872566868444670163)
XLA Ops:
  19.0 8.0 %all-to-all-done.2.ok.ov = bf16[4,2,2,128,256]{4,3,2,1,0:T(8,128)(2,1)S(1)} async-done(((bf16[4,2,2,128,256]{4,3,2,1,0:T(8,128)(2,1)}), bf16[4,2,2,128,256]{4,3,2,1,0:T(8,128)(2,1)S(1)}, u32[]{:S(2)}, u32[]{:S(2)}) %all-to-all-start.2) | async-done | bytes 1048608 | tf_op jit(solution)/shard_map/all_to_all | solution.py:424
  27.0 28.9 %all_to_all.75 = bf16[4,128,2048]{2,1,0:T(8,128)(2,1)} all-to-all(bf16[4,128,2048]{2,1,0:T(8,128)(2,1)S(1)} %get-tuple-element.14), channel_id=1, replica_groups=mesh['pipe'=8,'ctx'=4] {'ctx'}, dimensions={0} | all-to-all | bytes 4194304 | tf_op jit(solution)/shard_map/all_to_all | solution.py:424
  66.8 19.3 %all-to-all-done.12 = bf16[4,128,2048]{2,1,0:T(8,128)(2,1)} async-done(((bf16[4,128,2048]{2,1,0:T(8,128)(2,1)}), bf16[4,128,2048]{2,1,0:T(8,128)(2,1)}, u32[]{:S(2)}, u32[]{:S(2)}) %all-to-all-start.12) | async-done | bytes 2097184 | tf_op jit(solution)/shard_map/all_to_all | solution.py:424
  86.1 28.9 %all_to_all.76 = bf16[4,128,2048]{2,1,0:T(8,128)(2,1)} all-to-all(bf16[4,128,2048]{2,1,0:T(8,128)(2,1)S(1)} %get-tuple-element.10), channel_id=1, replica_groups=mesh['pipe'=8,'ctx'=4] {'ctx'}, dimensions={0} | all-to-all | bytes 4194304 | tf_op jit(solution)/shard_map/all_to_all | solution.py:424
  124.7 19.7 %all-to-all-done.8 = bf16[4,128,2048]{2,1,0:T(8,128)(2,1)S(1)} async-done(((bf16[4,128,2048]{2,1,0:T(8,128)(2,1)}), bf16[4,128,2048]{2,1,0:T(8,128)(2,1)S(1)}, u32[]{:S(2)}, u32[]{:S(2)}) %all-to-all-start.8) | async-done | bytes 2097184 | tf_op jit(solution)/shard_map/all_to_all | solution.py:424
  155.3 19.7 %all-to-all-done.4 = bf16[4,128,2048]{2,1,0:T(8,128)(2,1)S(1)} async-done(((bf16[4,128,2048]{2,1,0:T(8,128)(2,1)}), bf16[4,128,2048]{2,1,0:T(8,128)(2,1)S(1)}, u32[]{:S(2)}, u32[]{:S(2)}) %all-to-all-start.4) | async-done | bytes 2097184 | tf_op jit(solution)/shard_map/all_to_all | solution.py:424
  181.6 8.8 %project_kv.7 = bf16[4,512,512]{2,1,0:T(8,128)(2,1)} custom-call(bf16[512,2048]{1,0:T(8,128)(2,1)} %bitcast.28, bf16[1,2,2048,1024]{3,2,1,0:T(8,128)(2,1)} %key_ref.11, bf16[1,2,2048,1024]{3,2,1,0:T(8,128)(2,1)} %value_ref.11), custom_call_target="tpu_custom_call" | custom-call | flops 4294967296 | bytes 12582912 | tf_op jit(solution)/shard_map/project_kv/pallas_call | solution.py:90
  190.3 15.3 %all-to-all-done = bf16[4,128,2048]{2,1,0:T(8,128)(2,1)S(1)} async-done(((bf16[4,128,2048]{2,1,0:T(8,128)(2,1)}), bf16[4,128,2048]{2,1,0:T(8,128)(2,1)S(1)}, u32[]{:S(2)}, u32[]{:S(2)}) %all-to-all-start) | async-done | bytes 2097184 | tf_op jit(solution)/shard_map/all_to_all | solution.py:424
  213.0 8.7 %project_kv.6 = bf16[4,512,512]{2,1,0:T(8,128)(2,1)} custom-call(bf16[512,2048]{1,0:T(8,128)(2,1)} %bitcast.24, bf16[1,2,2048,1024]{3,2,1,0:T(8,128)(2,1)} %key_ref.11, bf16[1,2,2048,1024]{3,2,1,0:T(8,128)(2,1)} %value_ref.11), custom_call_target="tpu_custom_call" | custom-call | flops 4294967296 | bytes 12582912 | tf_op jit(solution)/shard_map/project_kv/pallas_call | solution.py:90
  221.7 15.4 %all-to-all-done.13.nk.nv = bf16[4,512,512]{2,1,0:T(8,128)(2,1)} async-done(((bf16[4,512,512]{2,1,0:T(8,128)(2,1)}), bf16[4,512,512]{2,1,0:T(8,128)(2,1)}, u32[]{:S(2)}, u32[]{:S(2)}) %all-to-all-start.13) | async-done | bytes 2097184 | tf_op jit(solution)/shard_map/all_to_all | solution.py:424
  243.2 8.7 %project_kv.5 = bf16[4,512,512]{2,1,0:T(8,128)(2,1)} custom-call(bf16[512,2048]{1,0:T(8,128)(2,1)} %bitcast.30, bf16[1,2,2048,1024]{3,2,1,0:T(8,128)(2,1)} %key_ref.11, bf16[1,2,2048,1024]{3,2,1,0:T(8,128)(2,1)} %value_ref.11), custom_call_target="tpu_custom_call" | custom-call | flops 4294967296 | bytes 12582912 | tf_op jit(solution)/shard_map/project_kv/pallas_call | solution.py:90
  252.0 15.4 %all-to-all-done.9.nk.nv = bf16[4,512,512]{2,1,0:T(8,128)(2,1)} async-done(((bf16[4,512,512]{2,1,0:T(8,128)(2,1)}), bf16[4,512,512]{2,1,0:T(8,128)(2,1)}, u32[]{:S(2)}, u32[]{:S(2)}) %all-to-all-start.9) | async-done | bytes 2097184 | tf_op jit(solution)/shard_map/all_to_all | solution.py:424
  273.5 26.5 %attend_back.3 = (bf16[512,2048]{1,0:T(8,128)(2,1)S(1)}, bf16[2,512,256]{2,1,0:T(8,128)(2,1)}) custom-call(s32[1,2,2]{2,1,0:T(2,128)S(1)} %copy-done.3, bf16[512,2048]{1,0:T(8,128)(2,1)} %bitcast.29, bf16[512,2048]{1,0:T(8,128)(2,1)} %bitcast.15.g_ref, bf16[4,512,512]{2,1,0:T(8,128)(2,1)} %all-to-all-done.13.nk.nv, ...), custom_call_target="tpu_custom_call" | custom-call | flops 10737418240 | bytes 8388608 | tf_op jit(solution)/shard_map/attend_back/pallas_call | solution.py:271
  301.5 8.7 %project_kv.4 = bf16[4,512,512]{2,1,0:T(8,128)(2,1)} custom-call(bf16[512,2048]{1,0:T(8,128)(2,1)} %bitcast.26, bf16[1,2,2048,1024]{3,2,1,0:T(8,128)(2,1)} %key_ref.11, bf16[1,2,2048,1024]{3,2,1,0:T(8,128)(2,1)} %value_ref.11), custom_call_target="tpu_custom_call" | custom-call | flops 4294967296 | bytes 12582912 | tf_op jit(solution)/shard_map/project_kv/pallas_call | solution.py:90
  314.9 19.4 %attend.3 = bf16[512,2048]{1,0:T(8,128)(2,1)} custom-call(s32[1,2,2]{2,1,0:T(2,128)S(1)} %copy-done.3, bf16[512,2048]{1,0:T(8,128)(2,1)} %bitcast.31, bf16[4,512,512]{2,1,0:T(8,128)(2,1)} %all-to-all-done.5.nk.nv, bf16[4,512,512]{2,1,0:T(8,128)(2,1)} %all-to-all-done.5.nk.nv, bf16[4,2,2,128,256]{4,3,2,1,0:T(8,128)(2,1)S(1)} %all-to-all-done.2.ok.ov, ...), custom_call_target="tpu_custom_call" | custom-call | flops 4294967296 | bytes 4194304 | tf_op jit(solution)/shard_map/attend/pallas_call | solution.py:260
  334.4 15.9 %all-to-all-done.1.nk.nv = bf16[4,512,512]{2,1,0:T(8,128)(2,1)} async-done(((bf16[4,512,512]{2,1,0:T(8,128)(2,1)}), bf16[4,512,512]{2,1,0:T(8,128)(2,1)}, u32[]{:S(2)}, u32[]{:S(2)}) %all-to-all-start.1) | async-done | bytes 2097184 | tf_op jit(solution)/shard_map/all_to_all | solution.py:424
  356.4 34.2 %attend_back.2 = (bf16[512,2048]{1,0:T(8,128)(2,1)S(1)}, bf16[2,512,256]{2,1,0:T(8,128)(2,1)}) custom-call(s32[1,2,2]{2,1,0:T(2,128)S(1)} %copy-done.3, bf16[512,2048]{1,0:T(8,128)(2,1)} %bitcast.25, bf16[512,2048]{1,0:T(8,128)(2,1)} %bitcast.32, bf16[4,512,512]{2,1,0:T(8,128)(2,1)} %all-to-all-done.9.nk.nv, bf16[4,512,512]{2,1,0:T(8,128)(2,1)} %all-to-all-done.9.nk.nv, ...), custom_call_target="tpu_custom_call" | custom-call | flops 10737418240 | bytes 8388608 | tf_op jit(solution)/shard_map/attend_back/pallas_call | solution.py:271
  392.1 19.4 %attend.2 = bf16[512,2048]{1,0:T(8,128)(2,1)} custom-call(s32[1,2,2]{2,1,0:T(2,128)S(1)} %copy-done.3, bf16[512,2048]{1,0:T(8,128)(2,1)} %bitcast.27, bf16[4,512,512]{2,1,0:T(8,128)(2,1)} %all-to-all-done.1.nk.nv, bf16[4,512,512]{2,1,0:T(8,128)(2,1)} %all-to-all-done.1.nk.nv, bf16[4,2,2,128,256]{4,3,2,1,0:T(8,128)(2,1)S(1)} %all-to-all-done.2.ok.ov, ...), custom_call_target="tpu_custom_call" | custom-call | flops 4294967296 | bytes 4194304 | tf_op jit(solution)/shard_map/attend/pallas_call | solution.py:260
  415.3 9.8 %back_rows.3 = bf16[512,2048]{1,0:T(8,128)(2,1)} custom-call(bf16[512,2048]{1,0:T(8,128)(2,1)} %copy-done.1, bf16[4,2,512,256]{3,2,1,0:T(8,128)(2,1)} %bitcast.33, bf16[1,2,2048,1024]{3,2,1,0:T(8,128)(2,1)} %key_ref.11, bf16[1,2,2048,1024]{3,2,1,0:T(8,128)(2,1)} %value_ref.11), custom_call_target="tpu_custom_call" | custom-call | flops 4294967296 | bytes 12582912 | tf_op jit(solution)/shard_map/back_rows/pallas_call | solution.py:307
  425.1 14.3 %all-to-all-done.3.attn_ref = bf16[4,128,2048]{2,1,0:T(8,128)(2,1)S(1)} async-done(((bf16[4,128,2048]{2,1,0:T(8,128)(2,1)}), bf16[4,128,2048]{2,1,0:T(8,128)(2,1)S(1)}, u32[]{:S(2)}, u32[]{:S(2)}) %all-to-all-start.3) | async-done | bytes 2097184 | tf_op jit(solution)/shard_map/all_to_all | solution.py:424
  446.8 9.8 %back_rows.2 = bf16[512,2048]{1,0:T(8,128)(2,1)} custom-call(bf16[512,2048]{1,0:T(8,128)(2,1)} %copy-done.2, bf16[4,2,512,256]{3,2,1,0:T(8,128)(2,1)} %bitcast.34, bf16[1,2,2048,1024]{3,2,1,0:T(8,128)(2,1)} %key_ref.11, bf16[1,2,2048,1024]{3,2,1,0:T(8,128)(2,1)} %value_ref.11), custom_call_target="tpu_custom_call" | custom-call | flops 4294967296 | bytes 12582912 | tf_op jit(solution)/shard_map/back_rows/pallas_call | solution.py:307
  456.6 14.4 %all-to-all-done.14.acts_ref = bf16[4,128,2048]{2,1,0:T(8,128)(2,1)} async-done(((bf16[4,128,2048]{2,1,0:T(8,128)(2,1)}), bf16[4,128,2048]{2,1,0:T(8,128)(2,1)}, u32[]{:S(2)}, u32[]{:S(2)}) %all-to-all-start.14) | async-done | bytes 2097184 | tf_op jit(solution)/shard_map/all_to_all | solution.py:424
  507.4 111.5 %collective-permute-done.1.refs_1_ = bf16[128,8192]{1,0:T(8,128)(2,1)} collective-permute-done((bf16[128,8192]{1,0:T(8,128)(2,1)S(1)}, bf16[128,8192]{1,0:T(8,128)(2,1)}, u32[]{:S(2)}, u32[]{:S(2)}) %collective-permute-start.1) | collective-permute-done | bytes 2097184 | tf_op jit(solution)/shard_map/ppermute | solution.py:420
  618.8 44.2 %collective-permute-done.refs_0_ = bf16[128,8192]{1,0:T(8,128)(2,1)} collective-permute-done((bf16[128,8192]{1,0:T(8,128)(2,1)}, bf16[128,8192]{1,0:T(8,128)(2,1)}, u32[]{:S(2)}, u32[]{:S(2)}) %collective-permute-start) | collective-permute-done | bytes 2097184 | tf_op jit(solution)/shard_map/ppermute | solution.py:420
  (58 shorter events, 140.3 us)
Async XLA Ops:
  9.1 5.1 copy-start
  10.2 16.8 %all-to-all-start.2 = ((bf16[4,2,2,128,256]{4,3,2,1,0:T(8,128)(2,1)}), bf16[4,2,2,128,256]{4,3,2,1,0:T(8,128)(2,1)S(1)}, u32[]{:S(2)}, u32[]{:S(2)}) async-start(bf16[4,2,2,128,256]{4,3,2,1,0:T(8,128)(2,1)} %pad_maximum_fusion.1), calls=%async_computation.2 | async-start | bytes 2097152 | tf_op jit(solution)/shard_map/all_to_all | solution.py:424
  55.9 30.2 %all-to-all-start.12 = ((bf16[4,128,2048]{2,1,0:T(8,128)(2,1)}), bf16[4,128,2048]{2,1,0:T(8,128)(2,1)}, u32[]{:S(2)}, u32[]{:S(2)}) async-start(bf16[4,128,2048]{2,1,0:T(8,128)(2,1)} %get-tuple-element.15), calls=%async_computation.12 | async-start | bytes 4194304 | tf_op jit(solution)/shard_map/all_to_all | solution.py:424
  115.1 29.3 %all-to-all-start.8 = ((bf16[4,128,2048]{2,1,0:T(8,128)(2,1)}), bf16[4,128,2048]{2,1,0:T(8,128)(2,1)S(1)}, u32[]{:S(2)}, u32[]{:S(2)}) async-start(bf16[4,128,2048]{2,1,0:T(8,128)(2,1)} %get-tuple-element.11), calls=%async_computation.8 | async-start | bytes 4194304 | tf_op jit(solution)/shard_map/all_to_all | solution.py:424
  145.7 29.3 %all-to-all-start.4 = ((bf16[4,128,2048]{2,1,0:T(8,128)(2,1)}), bf16[4,128,2048]{2,1,0:T(8,128)(2,1)S(1)}, u32[]{:S(2)}, u32[]{:S(2)}) async-start(bf16[4,128,2048]{2,1,0:T(8,128)(2,1)} %norm_rows.5), calls=%async_computation.4 | async-start | bytes 4194304 | tf_op jit(solution)/shard_map/all_to_all | solution.py:424
  175.0 1.4 copy-start.5
  176.3 29.3 %all-to-all-start = ((bf16[4,128,2048]{2,1,0:T(8,128)(2,1)}), bf16[4,128,2048]{2,1,0:T(8,128)(2,1)S(1)}, u32[]{:S(2)}, u32[]{:S(2)}) async-start(bf16[4,128,2048]{2,1,0:T(8,128)(2,1)} %norm_rows.4), calls=%async_computation | async-start | bytes 4194304 | tf_op jit(solution)/shard_map/all_to_all | solution.py:424
  206.9 30.2 %all-to-all-start.13 = ((bf16[4,512,512]{2,1,0:T(8,128)(2,1)}), bf16[4,512,512]{2,1,0:T(8,128)(2,1)}, u32[]{:S(2)}, u32[]{:S(2)}) async-start(bf16[4,512,512]{2,1,0:T(8,128)(2,1)} %project_kv.7), calls=%async_computation.13 | async-start | bytes 4194304 | tf_op jit(solution)/shard_map/all_to_all | solution.py:424
  237.2 30.2 %all-to-all-start.9 = ((bf16[4,512,512]{2,1,0:T(8,128)(2,1)}), bf16[4,512,512]{2,1,0:T(8,128)(2,1)}, u32[]{:S(2)}, u32[]{:S(2)}) async-start(bf16[4,512,512]{2,1,0:T(8,128)(2,1)} %project_kv.6), calls=%async_computation.9 | async-start | bytes 4194304 | tf_op jit(solution)/shard_map/all_to_all | solution.py:424
  252.0 21.5 %copy-start.3 = (s32[1,2,2]{2,1,0:T(2,128)S(1)}, s32[1,2,2]{2,1,0:T(2,128)}, u32[]{:S(2)}) copy-start(s32[1,2,2]{2,1,0:T(2,128)} %segment.7) | copy-start | bytes 52
  267.4 42.8 %all-to-all-start.5 = ((bf16[4,512,512]{2,1,0:T(8,128)(2,1)}), bf16[4,512,512]{2,1,0:T(8,128)(2,1)}, u32[]{:S(2)}, u32[]{:S(2)}) async-start(bf16[4,512,512]{2,1,0:T(8,128)(2,1)} %project_kv.5), calls=%async_computation.5 | async-start | bytes 4194304 | tf_op jit(solution)/shard_map/all_to_all | solution.py:424
  273.5 141.9 %all-gather.7.cloned.1.call-start = ((), (), s32[]{:S(2)}) async-start(), calls=%async_computation.16 | async-start | bytes 2621440 | tf_op jit(solution)/shard_map/all_gather | solution.py:486
  300.0 1.4 copy-start.1
  310.2 40.1 %all-to-all-start.1 = ((bf16[4,512,512]{2,1,0:T(8,128)(2,1)}), bf16[4,512,512]{2,1,0:T(8,128)(2,1)}, u32[]{:S(2)}, u32[]{:S(2)}) async-start(bf16[4,512,512]{2,1,0:T(8,128)(2,1)} %project_kv.4), calls=%async_computation.1 | async-start | bytes 4194304 | tf_op jit(solution)/shard_map/all_to_all | solution.py:424
  350.3 61.1 %all-to-all-start.6 = ((bf16[4,128,2048]{2,1,0:T(8,128)(2,1)}), bf16[4,128,2048]{2,1,0:T(8,128)(2,1)}, u32[]{:S(2)}, u32[]{:S(2)}) async-start(bf16[4,128,2048]{2,1,0:T(8,128)(2,1)} %bitcast.8), calls=%async_computation.6 | async-start | bytes 4194304 | tf_op jit(solution)/shard_map/all_to_all | solution.py:424
  356.4 90.4 %all-gather.5.cloned.1.call-start = ((), (), s32[]{:S(2)}) async-start(), calls=%async_computation.15 | async-start | bytes 2621440 | tf_op jit(solution)/shard_map/all_gather | solution.py:486
  390.6 1.4 copy-start.2
  411.4 27.9 %all-to-all-start.3 = ((bf16[4,128,2048]{2,1,0:T(8,128)(2,1)}), bf16[4,128,2048]{2,1,0:T(8,128)(2,1)S(1)}, u32[]{:S(2)}, u32[]{:S(2)}) async-start(bf16[4,128,2048]{2,1,0:T(8,128)(2,1)} %bitcast.6), calls=%async_computation.3 | async-start | bytes 4194304 | tf_op jit(solution)/shard_map/all_to_all | solution.py:424
  440.7 30.2 %all-to-all-start.14 = ((bf16[4,128,2048]{2,1,0:T(8,128)(2,1)}), bf16[4,128,2048]{2,1,0:T(8,128)(2,1)}, u32[]{:S(2)}, u32[]{:S(2)}) async-start(bf16[4,128,2048]{2,1,0:T(8,128)(2,1)} %bitcast.17), calls=%async_computation.14 | async-start | bytes 4194304 | tf_op jit(solution)/shard_map/all_to_all | solution.py:424
  470.9 30.5 %all-to-all-start.10 = ((bf16[4,128,2048]{2,1,0:T(8,128)(2,1)}), bf16[4,128,2048]{2,1,0:T(8,128)(2,1)}, u32[]{:S(2)}, u32[]{:S(2)}) async-start(bf16[4,128,2048]{2,1,0:T(8,128)(2,1)} %bitcast.13), calls=%async_computation.10 | async-start | bytes 4194304 | tf_op jit(solution)/shard_map/all_to_all | solution.py:424
  480.3 138.5 %collective-permute-start.1 = (bf16[128,8192]{1,0:T(8,128)(2,1)S(1)}, bf16[128,8192]{1,0:T(8,128)(2,1)}, u32[]{:S(2)}, u32[]{:S(2)}) collective-permute-start(bf16[128,8192]{1,0:T(8,128)(2,1)S(1)} %add_rows.3), channel_id=1, source_target_pairs={{0,4},{4,8},{8,12},{12,16},{16,20},{20,24},{24,28},{28,0},{1,5},{5... | collective-permute-start | bytes 6291464 | tf_op jit(solution)/shard_map/ppermute | solution.py:420
  484.7 178.3 %collective-permute-start = (bf16[128,8192]{1,0:T(8,128)(2,1)}, bf16[128,8192]{1,0:T(8,128)(2,1)}, u32[]{:S(2)}, u32[]{:S(2)}) collective-permute-start(bf16[128,8192]{1,0:T(8,128)(2,1)} %add_rows.2), channel_id=1, source_target_pairs={{0,4},{4,8},{8,12},{12,16},{16,20},{20,24},{24,28},{28,0},{1,5},{5... | collective-permute-start | bytes 6291464 | tf_op jit(solution)/shard_map/ppermute | solution.py:420
  493.7 174.0 %collective-permute-start.3 = (bf16[128,8192]{1,0:T(8,128)(2,1)}, bf16[128,8192]{1,0:T(8,128)(2,1)}, u32[]{:S(2)}, u32[]{:S(2)}) collective-permute-start(bf16[128,8192]{1,0:T(8,128)(2,1)} %grad_rows.3), channel_id=1, source_target_pairs={{0,28},{4,0},{8,4},{12,8},{16,12},{20,16},{24,20},{28,24},{1,29},{... | collective-permute-start | bytes 6291464 | tf_op jit(solution)/shard_map/ppermute | solution.py:420
  507.4 160.3 %collective-permute-start.2 = (bf16[128,8192]{1,0:T(8,128)(2,1)}, bf16[128,8192]{1,0:T(8,128)(2,1)}, u32[]{:S(2)}, u32[]{:S(2)}) collective-permute-start(bf16[128,8192]{1,0:T(8,128)(2,1)} %grad_rows.2), channel_id=1, source_target_pairs={{0,28},{4,0},{8,4},{12,8},{16,12},{20,16},{24,20},{28,24},{1,29},{... | collective-permute-start | bytes 6291464 | tf_op jit(solution)/shard_map/ppermute | solution.py:420
  (3 other events, 4.0 us)
Sparse Core Ops, SparseCore 0:
  301.6 40.9 all-gather.6
  392.2 23.3 all-gather.4
